TPU v7x, 32 devices: a whole 2x2x4 slice. The times are simulated.
32 devices in a mesh: seq: 32 (over z, y, x, core).
Axes of the slice: x: 2, y: 2, z: 4, core: 2. Of those that a mesh axis runs over, the one named last changes fastest.
Arguments:
- tokens: bfloat16 [16384, 1536], P('seq'), may hold values from -6 to 6
- norm_gain: float32 [1536], replicated, may hold values from 0.5 to 1.5
- w_query: bfloat16 [1536, 1536], replicated
- w_key_value: bfloat16 [1536, 256], replicated
- w_out: bfloat16 [1536, 1536], replicated, may hold values from -1.75 to 1.75
- segment_ids: int32 [16384], P('seq'), may hold values from 0 to 15, as said below
- page_owner: int32 [1024], P('seq'), may hold values from 0 to 31, as said below
- page_slot: int32 [1024], P('seq'), may hold values from 0 to 31, as said below
Outputs:
- attn_out: bfloat16 [16384, 1536], P('seq')
- kv_cache: bfloat16 [16384, 256], P('seq')
Inputs may be any that keep to these rules, and one draw needn't show every extreme that they name: `segment_ids`: segments are contiguous runs of the stream, never falling, each of 1 to 4096 tokens; one has exactly 4096. `page_owner`: the 32 pages of one device go to different owners; some owner keeps a page of every device. `page_slot`: two pages with the same owner have different slots.
All inputs are finite; a program needn't handle non-finite values.
Results may differ from a plain program's by a relative error of at most 0.0086.
Values may be sent and summed in bfloat16 or wider, within the bound.
A program may use at most 256 MiB of HBM per device.

v0:
```python
import jax
import jax.numpy as jnp
from jax import lax
from jax.sharding import PartitionSpec as P

WINDOW = 1024
PAGE = 16


EPS = 1e-06
ROPE_BASE = 10000.0


def carried_in(part, axis, combine, identity):
    place = lax.axis_index(axis)
    gathered = jax.tree.map(lambda a: lax.all_gather(a, axis), part)
    state = jax.tree.map(lambda a, e: jnp.zeros_like(a) + jnp.asarray(e, a.dtype), part, identity)

    def one(hop, state):
        return combine(
            state, jax.tree.map(lambda a: lax.dynamic_index_in_dim(a, hop, 0, False), gathered)
        )

    return lax.fori_loop(0, place, one, state)


def passed_along(value, axis, by):
    size = lax.axis_size(axis)
    pairs = [(i, i + by) for i in range(size) if 0 <= i + by < size]
    return lax.ppermute(value, axis, pairs)


def rotate(vectors, positions):
    width = vectors.shape[-1]
    half_dim = width // 2
    pair_index = jnp.arange(half_dim, dtype=jnp.float32)
    frequency = ROPE_BASE ** (-2.0 * pair_index / width)
    angles = positions.astype(jnp.float32)[:, None] * frequency[None, :]
    if vectors.ndim == 3:
        angles = angles[:, None, :]
    cosine = jnp.cos(angles)
    sine_part = jnp.sin(angles)
    first_half = vectors[..., :half_dim]
    second_half = vectors[..., half_dim:]
    return jnp.concatenate(
        [
            first_half * cosine - second_half * sine_part,
            second_half * cosine + first_half * sine_part,
        ],
        -1,
    )


def combine_runs(earlier, later):
    same_run = later[0] == earlier[0]
    missing = later[0] < 0
    run_id = jnp.where(missing, earlier[0], later[0])
    run_first = jnp.where(missing | same_run, earlier[1], later[1])
    return (run_id, run_first)


def body(tokens, norm_gain, w_query, w_key_value, w_out, segment_ids, page_owner, page_slot):
    row_count = tokens.shape[0]
    devices = lax.axis_size("seq")
    offset = lax.axis_index("seq") * row_count
    head_dim = w_key_value.shape[1] // 2
    head_count = w_query.shape[1] // head_dim
    local_index = jnp.arange(row_count, dtype=jnp.int32)
    global_index = offset + local_index
    change = jnp.concatenate([jnp.ones((1,), dtype=jnp.bool_), segment_ids[1:] != segment_ids[:-1]])
    local_start = lax.cummax(jnp.where(change, local_index, 0))
    last_run = (segment_ids[-1:], offset + local_start[-1:])
    empty_run = (jnp.full((1,), -1, jnp.int32), jnp.zeros((1,), jnp.int32))
    prior_id, prior_first = carried_in(last_run, "seq", combine_runs, empty_run)
    starts = jnp.where(segment_ids == prior_id, prior_first, offset + local_start)
    positions = global_index - starts
    wide = tokens.astype(jnp.float32)
    mean_square = jnp.mean(wide * wide, -1, keepdims=True)
    normed = (wide * lax.rsqrt(mean_square + EPS) * norm_gain).astype(jnp.bfloat16)
    queries = jnp.dot(normed, w_query, preferred_element_type=jnp.float32).reshape(
        row_count, head_count, head_dim
    )
    queries = (rotate(queries, positions) * head_dim ** (-0.5)).astype(jnp.bfloat16)
    projected = jnp.dot(normed, w_key_value, preferred_element_type=jnp.float32)
    keyval = jnp.concatenate(
        [rotate(projected[:, :head_dim], positions), projected[:, head_dim:]], 1
    ).astype(jnp.bfloat16)
    reach = WINDOW // row_count
    blocks = [keyval]
    moving = keyval
    for hop_step in range(reach):
        moving = passed_along(moving, "seq", 1)
        blocks.append(moving)
    ordered = blocks[::-1]
    block_firsts = [offset - (reach - place) * row_count for place in range(reach + 1)]

    def block_scores(block_rows, block_first):
        key_index = block_first + local_index
        valid = (
            (key_index[None, :] >= starts[:, None])
            & (key_index[None, :] <= global_index[:, None])
            & (global_index[:, None] - key_index[None, :] < WINDOW)
        )
        scores = jnp.einsum(
            "thd,kd->thk", queries, block_rows[:, :head_dim], preferred_element_type=jnp.float32
        )
        return jnp.where(valid[:, None, :], scores, -1e30)

    pieces = [block_scores(ordered[place], block_firsts[place]) for place in range(reach + 1)]
    scores = jnp.concatenate(pieces, 2)
    row_peak = jnp.max(scores, 2, keepdims=True)
    exponent = jnp.exp(scores - row_peak)
    probs = (exponent / jnp.sum(exponent, 2, keepdims=True)).astype(jnp.bfloat16)
    all_values = jnp.concatenate([block_rows[:, head_dim:] for block_rows in ordered], 0)
    context = jnp.einsum("thk,kd->thd", probs, all_values, preferred_element_type=jnp.float32)
    context = context.astype(jnp.bfloat16).reshape(row_count, head_count * head_dim)
    attn_out = jnp.dot(context, w_out, preferred_element_type=jnp.float32).astype(jnp.bfloat16)
    page_rows = keyval.reshape(row_count // PAGE, PAGE * 2 * head_dim)
    owner_hits = page_owner[:, None] == jnp.arange(devices, dtype=jnp.int32)[None, :]
    send_rows = jnp.einsum(
        "po,pc->oc", owner_hits.astype(jnp.bfloat16), page_rows, preferred_element_type=jnp.float32
    ).astype(jnp.bfloat16)
    send_slots = jnp.sum(jnp.where(owner_hits, page_slot[:, None] + 1, 0), 0) - 1
    got_rows, got_slots = (
        lax.all_to_all(send_rows, "seq", split_axis=0, concat_axis=0, tiled=True),
        lax.all_to_all(send_slots, "seq", split_axis=0, concat_axis=0, tiled=True),
    )
    placed = got_slots[None, :] == jnp.arange(devices, dtype=jnp.int32)[:, None]
    cache = jnp.dot(
        placed.astype(jnp.bfloat16), got_rows, preferred_element_type=jnp.float32
    ).astype(jnp.bfloat16)
    return (attn_out, cache.reshape(devices * PAGE, 2 * head_dim))


def solution(mesh):
    placed = (P("seq", None), P(), P(), P(), P(), P("seq"), P("seq"), P("seq"))
    return jax.shard_map(
        body,
        mesh=mesh,
        in_specs=placed,
        out_specs=(P("seq", None), P("seq", None)),
        check_vma=False,
    )
```

profile of v0, /device:TPU:0, one launch (start us, length us, event | category | flops | bytes accessed | tf_op | source)
XLA Modules:
  0.0 251.1 jit_solution(17083189321855266245)
XLA Ops:
  0.6 0.0 copy-start
  0.6 0.0 copy-start.3
  0.7 0.8 slice_compare_fusion
  1.5 0.1 add_select_fusion.1
  1.6 0.3 reduce-window.9
  1.9 0.1 slice.58
  2.0 0.1 slice_reduce_fusion
  2.1 0.1 maximum_bitcast_fusion.2
  2.2 0.8 slice_dynamic-update-slice_fusion
  3.1 0.2 add_dynamic-update-slice_fusion
  3.2 42.0 %all-reduce.2 = (s32[32]{0:T(128)S(1)}, s32[32]{0:T(128)S(1)}) all-reduce(s32[32]{0:T(128)S(1)} %slice_dynamic-update-slice_fusion, s32[32]{0:T(128)S(1)} %add_dynamic-update-slice_fusion), channel_id=2, replica_groups=mesh['seq'=32] {'seq'}, use_global_device_ids=true, to_apply=%add | all-reduce | flops 64 | bytes 512
  45.2 1.8 fusion.4
  47.0 0.0 copy-start.2
  47.0 2.3 fusion.12
  49.4 0.6 multiply_subtract_fusion.1
  50.0 4.3 %collective-permute-start = (bf16[512,256]{0,1:T(8,128)(2,1)S(1)}, bf16[512,256]{0,1:T(8,128)(2,1)S(1)}, u32[]{:S(2)}, u32[]{:S(2)}) collective-permute-start(bf16[512,256]{0,1:T(8,128)(2,1)S(1)} %maximum_convert_fusion), channel_id=1, source_target_pairs={{0,1},{1,2},{2,3},{3,4},{4,5},{5,6},{6,7},{7,8},{8,9},{9,10},{10,1... | collective-permute-start | bytes 786440 | tf_op jit(solution)/shard_map/ppermute | solution.py:30
  54.4 0.1 select_reduce_fusion
  54.5 0.7 copy.61
  55.1 106.5 %all-to-all-start = ((s32[32,1,1]{2,1,0:T(1,128)}), s32[32,1,1]{2,1,0:T(1,128)S(1)}, u32[]{:S(2)}, u32[]{:S(2)}) async-start(s32[32,1,1]{2,1,0:T(1,128)} %copy.61), calls=%async_computation | async-start | bytes 32768 | tf_op jit(solution)/shard_map/all_to_all | solution.py:126
  161.6 0.5 multiply_cosine_fusion
  162.2 0.1 copy.54
  162.3 0.1 copy.56
  162.4 4.8 %fusion.14 = f32[512,1536]{0,1:T(8,128)S(1)} fusion(bf16[1536,1536]{1,0:T(8,128)(2,1)} %param.12, bf16[512,1536]{1,0:T(8,128)(2,1)S(1)} %copy-done.2, f32[1536]{0:T(1024)S(1)} %copy-done.5, f32[512]{0:T(512)S(1)} %add_rsqrt_fusion), kind=kOutput, calls=%fused_computation.32 | convolution fusion | flops 2419064832 | bytes 9445376 | tf_op jit(solution)/shard_map/dot_general | solution.py:80
  167.2 1.4 fusion.26
  168.7 3.3 %copy.73 = f32[512,12,64]{2,0,1:T(8,128)} copy(f32[512,12,64]{0,2,1:T(8,128)} %get-tuple-element.59) | data formatting | bytes 3145728
  172.0 2.3 copy.74
  174.2 4.1 %multiply_subtract_fusion = (f32[512,12,64]{2,0,1:T(8,128)S(1)}, f32[512,12,64]{2,0,1:T(8,128)S(1)}) fusion(f32[512,12,64]{2,0,1:T(8,128)} %copy.74, f32[512,12,64]{2,0,1:T(8,128)} %copy.73, f32[512,64]{1,0:T(8,128)S(1)} %copy.56, f32[512,64]{1,0:T(8,128)S(1)} %copy.54), kind=kLoop, calls=%fused_computation.21 | loop fusion | flops 2359296 | bytes 6553600 | tf_op jit(solution)/shard_map/sub | solution.py:47
  178.3 0.9 fusion.7
  179.2 1.1 fusion.9
  180.3 6.5 %fusion.27 = (f32[512,12]{0,1:T(8,128)S(1)}, f32[512,12,512]{0,2,1:T(8,128)}) fusion(bf16[512,12,128]{2,0,1:T(8,128)(2,1)S(1)} %fusion.7, bf16[512,256]{0,1:T(8,128)(2,1)S(1)} %maximum_convert_fusion, pred[512,512]{0,1:T(8,128)(4,1)S(1)} %get-tuple-element.63), kind=kOutput, calls=%fused_computation.72 | convolution fusion | flops 811591680 | bytes 14573568 | tf_op jit(solution)/shard_map/thd,kd->thk/dot_general | solution.py:104
  186.8 0.1 copy.62
  186.9 0.1 convert_element_type.45
  187.1 0.3 fusion.3
  187.4 0.5 broadcast.265
  187.9 0.8 reduce.6
  188.7 0.9 reshape.363
  189.6 6.0 %all-to-all-start.1 = ((bf16[32,2,2048]{2,1,0:T(2,128)(2,1)}), bf16[32,2,2048]{2,1,0:T(2,128)(2,1)S(1)}, u32[]{:S(2)}, u32[]{:S(2)}) async-start(bf16[32,2,2048]{2,1,0:T(2,128)(2,1)} %reshape.363), calls=%async_computation.1 | async-start | bytes 524288 | tf_op jit(solution)/shard_map/all_to_all | solution.py:125
  195.6 0.7 reduce.4
  196.3 2.0 collective-permute-start.1
  198.3 6.4 %fusion.29 = (f32[512,12]{0,1:T(8,128)S(1)}, f32[512,12,512]{0,2,1:T(8,128)}) fusion(bf16[512,12,128]{2,0,1:T(8,128)(2,1)S(1)} %fusion.7, bf16[512,256]{0,1:T(8,128)(2,1)S(1)} %collective-permute-done, pred[512,512]{0,1:T(8,128)(4,1)S(1)} %get-tuple-element.64), kind=kOutput, calls=%fused_computation.74 | convolution fusion | flops 811591680 | bytes 14573568 | tf_op jit(solution)/shard_map/thd,kd->thk/dot_general | solution.py:104
  204.7 1.3 all-to-all-done.1
  206.0 0.3 reshape.364
  206.3 0.4 convolution_convert_fusion
  206.8 0.8 reshape.350
  207.6 6.5 %fusion.28 = (f32[512,12]{0,1:T(8,128)S(1)}, f32[512,12,512]{0,2,1:T(8,128)}) fusion(bf16[512,12,128]{2,0,1:T(8,128)(2,1)S(1)} %fusion.7, bf16[512,256]{0,1:T(8,128)(2,1)S(1)} %collective-permute-done.1, pred[512,512]{0,1:T(8,128)(4,1)S(1)} %get-tuple-element.62), kind=kOutput, calls=%fused_computation.73 | convolution fusion | flops 811591680 | bytes 14573568 | tf_op jit(solution)/shard_map/thd,kd->thk/dot_general | solution.py:104
  214.1 16.3 %fusion.1 = f32[512,12]{0,1:T(8,128)S(1)} fusion(f32[512,12,512]{0,2,1:T(8,128)} %get-tuple-element.68, f32[512,12,512]{0,2,1:T(8,128)} %get-tuple-element.72, f32[512,12,512]{0,2,1:T(8,128)} %get-tuple-element.70, f32[512,12]{0,1:T(8,128)S(1)} %maximum_maximum_fusion), kind=kLoop, calls=%fused_computation.5 | loop fusion | flops 37742592 | bytes 37797888 | tf_op jit(solution)/shard_map/reduce_sum | solution.py:113
  230.4 14.5 %fusion.8 = bf16[512,12,128]{0,2,1:T(8,128)(2,1)S(1)} fusion(f32[512,12,512]{0,2,1:T(8,128)} %get-tuple-element.68, f32[512,12,512]{0,2,1:T(8,128)} %get-tuple-element.72, f32[512,12,512]{0,2,1:T(8,128)} %get-tuple-element.70, f32[512,12]{0,1:T(8,128)S(1)} %fusion.1, f32[512,12]{0,1:T(8,128)S(1)} %maximum_maximum_fusion, bf16[512,128]{0,1:T(8,128)(2,1)S(1)} %slice.77, ...), kind=kOutput, calls=%fused_computation.23 | convolution fusion | flops 2465071104 | bytes 39763968 | tf_op jit(solution)/shard_map/thk,kd->thd/dot_general | solution.py:115
  245.0 6.1 %convolution_convert_fusion.2 = bf16[512,1536]{1,0:T(8,128)(2,1)} fusion(bf16[512,1536]{0,1:T(8,128)(2,1)S(1)} %bitcast.55, bf16[1536,1536]{1,0:T(8,128)(2,1)} %param.14), kind=kOutput, calls=%fused_computation.22 | convolution fusion | flops 2416705536 | bytes 7864320 | tf_op jit(solution)/shard_map/dot_general | solution.py:117
  (31 shorter events, 0.2 us)
Async XLA Ops:
  0.6 46.4 %copy-start = (bf16[1536,256]{1,0:T(8,128)(2,1)S(1)}, bf16[1536,256]{1,0:T(8,128)(2,1)}, u32[]{:S(2)}) copy-start(bf16[1536,256]{1,0:T(8,128)(2,1)} %param.13) | copy-start | bytes 2359300
  0.6 48.7 %copy-start.3 = (s32[512]{0:T(512)S(1)}, s32[512]{0:T(512)}, u32[]{:S(2)}) copy-start(s32[512]{0:T(512)} %param.15) | copy-start | bytes 6148
  45.2 9.2 %copy-start.6 = (s32[32]{0:T(128)S(1)}, s32[32]{0:T(128)}, u32[]{:S(2)}) copy-start(s32[32]{0:T(128)} %param.17) | copy-start | bytes 388
  45.2 9.2 %copy-start.4 = (s32[32]{0:T(128)S(1)}, s32[32]{0:T(128)}, u32[]{:S(2)}) copy-start(s32[32]{0:T(128)} %param.16) | copy-start | bytes 388
  47.0 115.4 %copy-start.2 = (bf16[512,1536]{1,0:T(8,128)(2,1)S(1)}, bf16[512,1536]{1,0:T(8,128)(2,1)}, u32[]{:S(2)}) copy-start(bf16[512,1536]{1,0:T(8,128)(2,1)} %param.10) | copy-start | bytes 4718596
  47.0 115.4 %copy-start.5 = (f32[1536]{0:T(1024)S(1)}, f32[1536]{0:T(1024)}, u32[]{:S(2)}) copy-start(f32[1536]{0:T(1024)} %param.11) | copy-start | bytes 18436
  50.0 146.3 %collective-permute-start = (bf16[512,256]{0,1:T(8,128)(2,1)S(1)}, bf16[512,256]{0,1:T(8,128)(2,1)S(1)}, u32[]{:S(2)}, u32[]{:S(2)}) collective-permute-start(bf16[512,256]{0,1:T(8,128)(2,1)S(1)} %maximum_convert_fusion), channel_id=1, source_target_pairs={{0,1},{1,2},{2,3},{3,4},{4,5},{5,6},{6,7},{7,8},{8,9},{9,10},{10,1... | collective-permute-start | bytes 786440 | tf_op jit(solution)/shard_map/ppermute | solution.py:30
  55.1 134.5 %all-to-all-start = ((s32[32,1,1]{2,1,0:T(1,128)}), s32[32,1,1]{2,1,0:T(1,128)S(1)}, u32[]{:S(2)}, u32[]{:S(2)}) async-start(s32[32,1,1]{2,1,0:T(1,128)} %copy.61), calls=%async_computation | async-start | bytes 32768 | tf_op jit(solution)/shard_map/all_to_all | solution.py:126
  189.6 16.4 %all-to-all-start.1 = ((bf16[32,2,2048]{2,1,0:T(2,128)(2,1)}), bf16[32,2,2048]{2,1,0:T(2,128)(2,1)S(1)}, u32[]{:S(2)}, u32[]{:S(2)}) async-start(bf16[32,2,2048]{2,1,0:T(2,128)(2,1)} %reshape.363), calls=%async_computation.1 | async-start | bytes 524288 | tf_op jit(solution)/shard_map/all_to_all | solution.py:125
  196.3 11.3 %collective-permute-start.1 = (bf16[512,256]{0,1:T(8,128)(2,1)S(1)}, bf16[512,256]{0,1:T(8,128)(2,1)S(1)}, u32[]{:S(2)}, u32[]{:S(2)}) collective-permute-start(bf16[512,256]{0,1:T(8,128)(2,1)S(1)} %collective-permute-done), channel_id=1, source_target_pairs={{0,1},{1,2},{2,3},{3,4},{4,5},{5,6},{6,7},{7,8},{8,9},{9,10},{10,1... | collective-permute-start | bytes 786440 | tf_op jit(solution)/shard_map/ppermute | solution.py:30
  245.0 6.2 %copy-start.1 = (bf16[1536,256]{1,0:T(8,128)(2,1)S(1)}, bf16[1536,256]{1,0:T(8,128)(2,1)}, u32[]{:S(2)}) copy-start(bf16[1536,256]{1,0:T(8,128)(2,1)} %param.13) | copy-start | bytes 2359300
where the time goes:
time: 253 us; the launch traced here: 251 us
  starting transfers between devices  119 us (47%)
  matrix products  47.9 us (19%)
  blocking collectives  42 us (17%)
  other arithmetic  28.4 us (11%)
  local copies, waits for them, and re-layouts  11.8 us (5%)
    all_to_all x1, starting transfers between devices, body(): lax.all_to_all(send_slots, 'seq', split_axis=0, concat_axis=0, tiled=True)  106 us
    unnamed x1, blocking collectives  42 us
    dot_general x3, matrix products, block_scores(): jnp.einsum('thd,kd->thk', queries, block_rows[:, :head_dim], preferred_el...  19.4 us
    reduce_sum x1, other arithmetic, body(): jnp.sum(exponent, 2, keepdims=True)  16.3 us
    dot_general x1, matrix products, body(): jnp.einsum('thk,kd->thd', probs, all_values, preferred_element_type=jnp.f...  14.5 us
    unnamed x21, local copies, waits for them, and re-layouts  7.6 us
    ppermute x2, starting transfers between devices, passed_along(): return lax.ppermute(value, axis, pairs)  6.34 us
    dot_general x1, matrix products, body(): jnp.dot(context, w_out, preferred_element_type=jnp.float32)  6.14 us
  transfers between devices with their start and end apart: 4, of which 1 were waited for; matrix products, arithmetic and copies ran while one was open for 15% of the time, Pallas kernels for 0%

commit v1 on v0

v1 whole, which is shorter than its diff:
```python
import functools
import math

import jax
import jax.numpy as jnp
import numpy as np
from jax import lax
from jax.experimental import pallas as pl
from jax.experimental.pallas import tpu as pltpu
from jax.sharding import PartitionSpec as P

WINDOW = 1024
MAXLEN = 4096
PAGE = 16
EPS = 1e-06
ROPE_BASE = 10000.0
LANES = 128
QUERY_TILE = 128
HEAD_GROUP = 4
MESH = pl.DeviceIdType.MESH


def cos_sin(angles):
    turns = jnp.floor(angles * (2.0 / math.pi) + 0.5)
    c1 = 1.5703125
    c2 = float(np.float32(4.837512969970703125e-4))
    c3 = float(np.float32(7.54978995489188216e-8))
    r = ((angles - turns * c1) - turns * c2) - turns * c3
    r2 = r * r
    s = r * (1.0 + r2 * (-1.0 / 6 + r2 * (1.0 / 120 + r2 * (-1.0 / 5040))))
    c = 1.0 + r2 * (-0.5 + r2 * (1.0 / 24 + r2 * (-1.0 / 720 + r2 * (1.0 / 40320))))
    quadrant = turns.astype(jnp.int32) & 3
    odd = (quadrant & 1) == 1
    cosine = jnp.where(odd, s, c)
    sine = jnp.where(odd, c, s)
    cosine = jnp.where((quadrant == 1) | (quadrant == 2), -cosine, cosine)
    sine = jnp.where(quadrant >= 2, -sine, sine)
    return cosine, sine


def column_of(row):
    shape = (LANES, LANES)
    diagonal = lax.broadcasted_iota(jnp.int32, shape, 0) == lax.broadcasted_iota(jnp.int32, shape, 1)
    return jnp.sum(jnp.where(diagonal, jnp.broadcast_to(row, shape), 0), 1, keepdims=True)


def spread(column, count):
    shape = (count, count * PAGE)
    lane = lax.broadcasted_iota(jnp.int32, shape, 1)
    mine = (lane // PAGE) == lax.broadcasted_iota(jnp.int32, shape, 0)
    row = jnp.sum(jnp.where(mine, column, 0), 0, keepdims=True)
    return row * PAGE + lax.broadcasted_iota(jnp.int32, (1, count * PAGE), 1) % PAGE


def one_hot_rows(targets, first, rows):
    row = first + lax.broadcasted_iota(jnp.int32, (rows, targets.shape[1]), 0)
    return jnp.where(row == targets, 1.0, 0.0).astype(jnp.bfloat16)


def exchange_kernel(
    devices, pages, reach, back,
    table_ref, frequency_ref, gain_ref, tokens_ref, w_kv_ref, w_query_ref,
    query_out, kv_out, low_out, cache_out,
    tokens_buf, w_kv_buf, w_query_buf, normed, kv_own, kv_in, tables, send_pages, got_pages,
    cosine, sine, load_sem, table_send, table_recv, page_send, page_recv, kv_send, kv_recv,
):
    me = lax.axis_index("seq")
    rows = tokens_buf.shape[0]
    head_dim = kv_own.shape[1] // 2
    seg_rows = rows // LANES
    loads = [
        pltpu.make_async_copy(tokens_ref, tokens_buf, load_sem.at[0]),
        pltpu.make_async_copy(w_kv_ref, w_kv_buf, load_sem.at[1]),
        pltpu.make_async_copy(w_query_ref, w_query_buf, load_sem.at[2]),
    ]
    for load in loads:
        load.start()

    barrier = pltpu.get_barrier_semaphore()

    def greet(k, carry):
        pl.semaphore_signal(
            barrier, inc=1, device_id=(lax.rem(me + k, devices),), device_id_type=MESH
        )
        return carry

    lax.fori_loop(1, devices, greet, 0)
    pl.semaphore_wait(barrier, devices - 1)

    def send_table(k, carry):
        pltpu.make_async_remote_copy(
            src_ref=table_ref, dst_ref=tables.at[k - 1], send_sem=table_send, recv_sem=table_recv,
            device_id=(lax.rem(me + k, devices),), device_id_type=MESH,
        ).start()
        return carry

    lax.fori_loop(1, devices, send_table, 0)
    tables[devices - 1] = table_ref[...]

    loads[0].wait()
    step = 128

    def norm_tile(i, carry):
        at = pl.ds(pl.multiple_of(i * step, step), step)
        wide = tokens_buf[at, :].astype(jnp.float32)
        mean_square = jnp.mean(wide * wide, -1, keepdims=True)
        normed[at, :] = (wide * lax.rsqrt(mean_square + EPS) * gain_ref[...]).astype(jnp.bfloat16)
        return carry

    lax.fori_loop(0, rows // step, norm_tile, 0)
    loads[1].wait()
    projected = jnp.dot(normed[...], w_kv_buf[...], preferred_element_type=jnp.float32)

    table = table_ref[...]
    ids = jnp.concatenate([column_of(table[r : r + 1, :]) for r in range(seg_rows)], 0)
    below = jnp.zeros((rows, LANES), jnp.int32)
    for r in range(seg_rows):
        below = below + jnp.where(table[r : r + 1, :] < ids, 1, 0)
    local_start = jnp.sum(below, 1, keepdims=True)
    owner_column = column_of(table[seg_rows : seg_rows + 1, :])[:pages]
    order = one_hot_rows(spread(owner_column, pages), 0, devices * PAGE)

    blocks = tables.at[pl.ds(0, devices - 1)]
    pltpu.make_async_copy(blocks, blocks, table_recv).wait()
    first_id = table[0:1, 0:1]
    earlier = jnp.zeros((seg_rows, LANES), jnp.int32)
    for k in range(1, min(back, devices - 1) + 1):
        present = jnp.where(me >= k, 1, 0)
        earlier = earlier + jnp.where(tables[k - 1, 0:seg_rows, :] == first_id, present, 0)
    before = jnp.sum(jnp.sum(earlier, 1, keepdims=True), 0, keepdims=True)
    local_index = lax.broadcasted_iota(jnp.int32, (rows, 1), 0)
    start = local_start - jnp.where(ids == first_id, before, 0)
    positions = local_index - start
    low = jnp.maximum(start, local_index - (WINDOW - 1)) + reach * rows
    low_out[...] = jnp.broadcast_to(low, low_out.shape)

    angles = positions.astype(jnp.float32) * frequency_ref[...]
    cos_part, sin_part = cos_sin(angles)
    lane = lax.broadcasted_iota(jnp.int32, (rows, head_dim), 1)
    cosine[...] = cos_part
    sine[...] = jnp.where(lane < head_dim // 2, -sin_part, sin_part)

    def rotate(v):
        return v * cosine[...] + pltpu.roll(v, head_dim // 2, 1) * sine[...]

    kv_own[:, :head_dim] = rotate(projected[:, :head_dim]).astype(jnp.bfloat16)
    kv_own[:, head_dim:] = projected[:, head_dim:].astype(jnp.bfloat16)
    kv_copies = []
    for hop in range(1, reach + 1):
        copy = pltpu.make_async_remote_copy(
            src_ref=kv_own, dst_ref=kv_in.at[reach - hop],
            send_sem=kv_send.at[hop - 1], recv_sem=kv_recv.at[hop - 1],
            device_id=(lax.rem(me + hop, devices),), device_id_type=MESH,
        )
        copy.start()
        kv_copies.append(copy)
    send_pages[...] = (
        jnp.dot(order, kv_own[...], preferred_element_type=jnp.float32)
        .astype(jnp.bfloat16)
        .reshape(send_pages.shape)
    )

    def send_page(k, carry):
        to = lax.rem(me + k, devices)
        pltpu.make_async_remote_copy(
            src_ref=send_pages.at[to], dst_ref=got_pages.at[k - 1],
            send_sem=page_send, recv_sem=page_recv,
            device_id=(to,), device_id_type=MESH,
        ).start()
        return carry

    lax.fori_loop(1, devices, send_page, 0)
    got_pages[devices - 1] = send_pages[me]

    loads[2].wait()
    pair = 2 * head_dim
    scale = head_dim ** (-0.5) * math.log2(math.e)

    def query_pair(j, carry):
        columns = pl.ds(pl.multiple_of(j * pair, pair), pair)
        part = jnp.dot(normed[...], w_query_buf[:, columns], preferred_element_type=jnp.float32)
        query_out[2 * j] = (rotate(part[:, :head_dim]) * scale).astype(jnp.bfloat16)
        query_out[2 * j + 1] = (rotate(part[:, head_dim:]) * scale).astype(jnp.bfloat16)
        return carry

    lax.fori_loop(0, query_out.shape[0] // 2, query_pair, 0)

    kv_out[reach * rows :, :] = kv_own[...]
    owners = tables[:, seg_rows, :]
    slots = tables[:, seg_rows + 1, :]
    slot_column = jnp.sum(jnp.where(owners == me, slots + 1, 0), 1, keepdims=True) - 1
    targets = spread(slot_column, devices)

    pages_in = got_pages.at[pl.ds(0, devices - 1)]
    pltpu.make_async_copy(pages_in, pages_in, page_recv).wait()
    got = got_pages[...].reshape(devices * PAGE, 2 * head_dim)
    chunk = min(512, cache_out.shape[0])
    for c in range(cache_out.shape[0] // chunk):
        place = one_hot_rows(targets, c * chunk, chunk)
        cache_out[c * chunk : (c + 1) * chunk, :] = jnp.dot(
            place, got, preferred_element_type=jnp.float32
        ).astype(jnp.bfloat16)
    for hop in range(1, reach + 1):
        kv_copies[hop - 1].wait()
    for slot in range(reach):
        kv_out[slot * rows : (slot + 1) * rows, :] = kv_in[slot]
    pltpu.make_async_copy(blocks, blocks, table_send).wait()
    pltpu.make_async_copy(pages_in, pages_in, page_send).wait()


def attention_kernel(query_ref, kv_ref, low_ref, w_out_ref, out_ref, context, value_sum, bias, w_buf, sem):
    heads, rows, head_dim = query_ref.shape
    load = pltpu.make_async_copy(w_out_ref, w_buf, sem)
    load.start()
    span = WINDOW + QUERY_TILE
    value_sum[:, :head_dim] = kv_ref[:, head_dim:]
    value_sum[:, head_dim:] = jnp.ones((kv_ref.shape[0], head_dim), jnp.bfloat16)
    extra = kv_ref.shape[0] - rows

    def tile(i, carry):
        first = pl.multiple_of(i * QUERY_TILE, QUERY_TILE)
        at = pl.ds(first, QUERY_TILE)
        shape = (QUERY_TILE, span)
        key_row = first + (extra - WINDOW) + lax.broadcasted_iota(jnp.int32, shape, 1)
        query_row = first + extra + lax.broadcasted_iota(jnp.int32, shape, 0)
        low = low_ref[at, 0:1]
        bias[...] = jnp.where((key_row >= low) & (key_row <= query_row), 0.0, -1e30)
        key_at = pl.ds(pl.multiple_of(first + (extra - WINDOW), QUERY_TILE), span)

        def group(g, carry):
            for j in range(HEAD_GROUP):
                h = g * HEAD_GROUP + j
                scores = lax.dot_general(
                    query_ref[h, at, :], kv_ref[key_at, :head_dim],
                    (((1,), (1,)), ((), ())), preferred_element_type=jnp.float32,
                ) + bias[...]
                peak = jnp.max(scores, 1, keepdims=True)
                weights = jnp.exp2(scores - peak).astype(jnp.bfloat16)
                both = jnp.dot(weights, value_sum[key_at, :], preferred_element_type=jnp.float32)
                context[h, at, :] = (both[:, :head_dim] / both[:, head_dim:]).astype(jnp.bfloat16)
            return carry

        lax.fori_loop(0, heads // HEAD_GROUP, group, 0)
        return carry

    lax.fori_loop(0, rows // QUERY_TILE, tile, 0)
    load.wait()
    whole = jnp.concatenate([context[h] for h in range(heads)], 1)
    width = 256

    def column(j, carry):
        columns = pl.ds(pl.multiple_of(j * width, width), width)
        out_ref[:, columns] = jnp.dot(
            whole, w_buf[:, columns], preferred_element_type=jnp.float32
        ).astype(jnp.bfloat16)
        return carry

    lax.fori_loop(0, out_ref.shape[1] // width, column, 0)


def body(devices, tokens, norm_gain, w_query, w_key_value, w_out, segment_ids, page_owner, page_slot):
    rows, width = tokens.shape
    head_dim = w_key_value.shape[1] // 2
    heads = w_query.shape[1] // head_dim
    pages = rows // PAGE
    reach = WINDOW // rows
    back = MAXLEN // rows
    bf16, f32 = jnp.bfloat16, jnp.float32
    pad = jnp.full((LANES - pages,), -1, jnp.int32)
    seg_rows = rows // LANES
    table = jnp.concatenate(
        [segment_ids, page_owner, pad, page_slot, pad, jnp.zeros(((6 - seg_rows) * LANES,), jnp.int32)]
    ).reshape(8, LANES)
    half = ROPE_BASE ** (-2.0 * np.arange(head_dim // 2, dtype=np.float64) / head_dim)
    frequency = jnp.asarray(np.concatenate([half, half])[None, :].astype(np.float32))
    vmem = pl.BlockSpec(memory_space=pltpu.VMEM)
    anywhere = pl.BlockSpec(memory_space=pl.ANY)
    dma = pltpu.SemaphoreType.DMA
    query, kv_all, low, cache = pl.pallas_call(
        functools.partial(exchange_kernel, devices, pages, reach, back),
        out_shape=(
            jax.ShapeDtypeStruct((heads, rows, head_dim), bf16),
            jax.ShapeDtypeStruct(((reach + 1) * rows, 2 * head_dim), bf16),
            jax.ShapeDtypeStruct((rows, LANES), jnp.int32),
            jax.ShapeDtypeStruct((devices * PAGE, 2 * head_dim), bf16),
        ),
        in_specs=[vmem, vmem, vmem, anywhere, anywhere, anywhere],
        out_specs=(vmem, vmem, vmem, vmem),
        scratch_shapes=[
            pltpu.VMEM((rows, width), bf16),
            pltpu.VMEM(w_key_value.shape, bf16),
            pltpu.VMEM(w_query.shape, bf16),
            pltpu.VMEM((rows, width), bf16),
            pltpu.VMEM((rows, 2 * head_dim), bf16),
            pltpu.VMEM((reach, rows, 2 * head_dim), bf16),
            pltpu.VMEM((devices, 8, LANES), jnp.int32),
            pltpu.VMEM((devices, PAGE, 2 * head_dim), bf16),
            pltpu.VMEM((devices, PAGE, 2 * head_dim), bf16),
            pltpu.VMEM((rows, head_dim), f32),
            pltpu.VMEM((rows, head_dim), f32),
            dma((3,)),
            dma, dma, dma, dma,
            dma((reach,)), dma((reach,)),
        ],
        compiler_params=pltpu.CompilerParams(
            collective_id=0, has_side_effects=True, vmem_limit_bytes=48 * 1024 * 1024
        ),
        name="project_and_exchange",
    )(table, frequency, norm_gain.reshape(1, width), tokens, w_key_value, w_query)
    attn_out = pl.pallas_call(
        attention_kernel,
        out_shape=jax.ShapeDtypeStruct((rows, w_out.shape[1]), bf16),
        in_specs=[vmem, vmem, vmem, anywhere],
        out_specs=vmem,
        scratch_shapes=[
            pltpu.VMEM((heads, rows, head_dim), bf16),
            pltpu.VMEM(((reach + 1) * rows, 2 * head_dim), bf16),
            pltpu.VMEM((QUERY_TILE, WINDOW + QUERY_TILE), f32),
            pltpu.VMEM(w_out.shape, bf16),
            dma,
        ],
        compiler_params=pltpu.CompilerParams(vmem_limit_bytes=48 * 1024 * 1024),
        name="attend_and_project",
    )(query, kv_all, low, w_out)
    return attn_out, cache


def solution(mesh):
    placed = (P("seq", None), P(), P(), P(), P(), P("seq"), P("seq"), P("seq"))
    return jax.shard_map(
        functools.partial(body, mesh.shape["seq"]),
        mesh=mesh,
        in_specs=placed,
        out_specs=(P("seq", None), P("seq", None)),
        check_vma=False,
    )
```

time: 253 us -> 56.6 us (0.22)
  starting transfers between devices: 119 us -> 0 us
  Pallas kernels: 0 us -> 50.3 us
  matrix products: 47.9 us -> 0 us
  blocking collectives: 42 us -> 0 us
  other arithmetic: 28.4 us -> 0 us
  local copies, waits for them, and re-layouts: 11.8 us -> 5.37 us
    all_to_all x2 -> x0, starting transfers between devices: 112 us -> none  [the longest x1 106 us: body(): lax.all_to_all(send_slots, 'seq', split_axis=0, concat_axis=0, tiled=True)]
    pallas_call x0 -> x2, Pallas kernels: none -> 50.3 us  [the longest x1 28.8 us: body(): pl.pallas_call(functools.partial(exchange_kernel, devices, pages, reach,...]
    dot_general x9 -> x0, matrix products: 47.9 us -> none  [the longest x3 19.4 us: block_scores(): jnp.einsum('thd,kd->thk', queries, block_rows[:, :head_dim], preferred_el...]
    unnamed x1 -> x0, blocking collectives: 42 us -> none
    reduce_sum x3 -> x0, other arithmetic: 18.2 us -> none  [the longest x1 16.3 us: body(): jnp.sum(exponent, 2, keepdims=True)]
    ppermute x2 -> x0, starting transfers between devices: 6.34 us -> none  [passed_along(): return lax.ppermute(value, axis, pairs)]
    sub x3 -> x0, other arithmetic: 4.62 us -> none  [the longest x2 4.62 us: rotate(): first_half * cosine - second_half * sine_part]
    unnamed x21 -> x7, local copies, waits for them, and re-layouts: 7.6 us -> 3.9 us
  transfers between devices with their start and end apart: 4 -> 0, of which waited for: 1 -> 0; matrix products, arithmetic and copies ran while one was open for 15% -> 0% of each run, Pallas kernels for 0% -> 0%
where the time goes in v1:
time: 56.6 us; the launch traced here: 56.4 us
  Pallas kernels  50.3 us (89%)
  local copies, waits for them, and re-layouts  5.37 us (9%)
  between operations  0.66 us (1%)
    pallas_call x1, Pallas kernels, body(): pl.pallas_call(functools.partial(exchange_kernel, devices, pages, reach,...  28.8 us
    pallas_call x1, Pallas kernels, body(): pl.pallas_call(attention_kernel, out_shape=jax.ShapeDtypeStruct((rows, w_...  21.6 us
    unnamed x7, local copies, waits for them, and re-layouts  3.9 us

profile of v1, /device:TPU:0, one launch (start us, length us, event | category | flops | bytes accessed | tf_op | source)
XLA Modules:
  0.0 56.4 jit_solution(302536994865307118)
XLA Ops:
  0.6 0.8 %concatenate.3 = s32[1024]{0:T(1024)S(1)} concatenate(s32[512]{0:T(512)} %param.14, s32[32]{0:T(128)} %param.15, s32[96]{0:T(128)S(1)} %broadcast_in_dim.6, s32[32]{0:T(128)} %param.16, s32[96]{0:T(128)S(1)} %broadcast_in_dim.6, s32[256]{0:T(256)S(1)} %broadcast_in_dim.7), dimensions={0} | concatenate | bytes 8192 | tf_op jit(solution)/shard_map/concatenate | solution.py:271
  1.4 0.7 %reshape.11.gain_ref = f32[1,1536]{1,0:T(1,128)S(1)} reshape(f32[1536]{0:T(1024)} %param.10) | data formatting | bytes 12288 | tf_op jit(solution)/shard_map/reshape | solution.py:309
  2.1 0.0 copy-start
  2.1 1.4 %copy-done = bf16[512,1536]{1,0:T(8,128)(2,1)S(1)} copy-done((bf16[512,1536]{1,0:T(8,128)(2,1)S(1)}, bf16[512,1536]{1,0:T(8,128)(2,1)}, u32[]{:S(2)}) %copy-start) | copy-done | bytes 1572888
  3.5 0.0 copy-start.1
  3.5 1.1 %copy-done.1 = bf16[1536,256]{1,0:T(8,128)(2,1)S(1)} copy-done((bf16[1536,256]{1,0:T(8,128)(2,1)S(1)}, bf16[1536,256]{1,0:T(8,128)(2,1)}, u32[]{:S(2)}) %copy-start.1) | copy-done | bytes 786456
  4.7 0.0 copy-start.2
  4.7 0.7 %copy-done.2 = f32[1,128]{1,0:T(1,128)S(1)} copy-done((f32[1,128]{1,0:T(1,128)S(1)}, f32[1,128]{1,0:T(1,128)}, u32[]{:S(2)}) %copy-start.2) | copy-done | bytes 536
  5.3 28.8 %project_and_exchange.1 = (bf16[12,512,128]{2,1,0:T(8,128)(2,1)S(1)}, bf16[1536,256]{1,0:T(8,128)(2,1)S(1)}, s32[512,128]{1,0:T(8,128)S(1)}, bf16[512,256]{1,0:T(8,128)(2,1)S(1)}) custom-call(s32[8,128]{1,0:T(8,128)S(1)} %bitcast.1, f32[1,128]{1,0:T(1,128)S(1)} %copy-done.2, f32[1,1536]{1,0:T(1,128)S(1)} %reshape.11.gain_ref, bf16[512,1536]{1,0:T(8,128)(2,1)S(1)} %copy-done, ...), custom_call_target="tpu_custom_call" | custom-call | tf_op jit(solution)/shard_map/project_and_exchange/pallas_call | solution.py:279
  34.1 21.6 %attend_and_project.1 = bf16[512,1536]{1,0:T(8,128)(2,1)} custom-call(bf16[12,512,128]{2,1,0:T(8,128)(2,1)S(1)} %get-tuple-element.6.query_ref, bf16[1536,256]{1,0:T(8,128)(2,1)S(1)} %get-tuple-element.7.kv_ref, s32[512,128]{1,0:T(8,128)S(1)} %get-tuple-element.8.low_ref, bf16[1536,1536]{1,0:T(8,128)(2,1)} %w_out_ref.1), custom_call_target="tpu_custom_call" | custom-call | tf_op jit(solution)/shard_map/attend_and_project/pallas_call | solution.py:310
  55.7 0.7 %copy.12 = bf16[512,256]{1,0:T(8,128)(2,1)} copy(bf16[512,256]{1,0:T(8,128)(2,1)S(1)} %get-tuple-element.13) | data formatting | bytes 524288
  (2 shorter events, 0.0 us)
Async XLA Ops:
  2.1 1.4 %copy-start = (bf16[512,1536]{1,0:T(8,128)(2,1)S(1)}, bf16[512,1536]{1,0:T(8,128)(2,1)}, u32[]{:S(2)}) copy-start(bf16[512,1536]{1,0:T(8,128)(2,1)} %tokens_ref.1) | copy-start | bytes 4718596
  3.5 1.1 %copy-start.1 = (bf16[1536,256]{1,0:T(8,128)(2,1)S(1)}, bf16[1536,256]{1,0:T(8,128)(2,1)}, u32[]{:S(2)}) copy-start(bf16[1536,256]{1,0:T(8,128)(2,1)} %w_kv_ref.1) | copy-start | bytes 2359300
  4.7 0.7 %copy-start.2 = (f32[1,128]{1,0:T(1,128)S(1)}, f32[1,128]{1,0:T(1,128)}, u32[]{:S(2)}) copy-start(f32[1,128]{1,0:T(1,128)} %constant.6.clone.frequency_ref) | copy-start | bytes 1540

commit v2 on v1

v2 whole, which is shorter than its diff:
```python
import functools
import math

import jax
import jax.numpy as jnp
import numpy as np
from jax import lax
from jax.experimental import pallas as pl
from jax.experimental.pallas import tpu as pltpu
from jax.sharding import PartitionSpec as P

WINDOW = 1024
MAXLEN = 4096
PAGE = 16
EPS = 1e-06
ROPE_BASE = 10000.0
LANES = 128
QUERY_TILE = 128
HEAD_GROUP = 2
MESH = pl.DeviceIdType.MESH


def cos_sin(angles):
    turns = jnp.floor(angles * (2.0 / math.pi) + 0.5)
    c1 = 1.5703125
    c2 = float(np.float32(4.837512969970703125e-4))
    c3 = float(np.float32(7.54978995489188216e-8))
    r = ((angles - turns * c1) - turns * c2) - turns * c3
    r2 = r * r
    s = r * (1.0 + r2 * (-1.0 / 6 + r2 * (1.0 / 120 + r2 * (-1.0 / 5040))))
    c = 1.0 + r2 * (-0.5 + r2 * (1.0 / 24 + r2 * (-1.0 / 720 + r2 * (1.0 / 40320))))
    quadrant = turns.astype(jnp.int32) & 3
    odd = (quadrant & 1) == 1
    cosine = jnp.where(odd, s, c)
    sine = jnp.where(odd, c, s)
    cosine = jnp.where((quadrant == 1) | (quadrant == 2), -cosine, cosine)
    sine = jnp.where(quadrant >= 2, -sine, sine)
    return cosine, sine


def column_of(row):
    shape = (LANES, LANES)
    diagonal = lax.broadcasted_iota(jnp.int32, shape, 0) == lax.broadcasted_iota(jnp.int32, shape, 1)
    return jnp.sum(jnp.where(diagonal, jnp.broadcast_to(row, shape), 0), 1, keepdims=True)


def spread(column, count):
    shape = (count, count * PAGE)
    lane = lax.broadcasted_iota(jnp.int32, shape, 1)
    mine = (lane // PAGE) == lax.broadcasted_iota(jnp.int32, shape, 0)
    row = jnp.sum(jnp.where(mine, column, 0), 0, keepdims=True)
    return row * PAGE + lax.broadcasted_iota(jnp.int32, (1, count * PAGE), 1) % PAGE


def one_hot_rows(targets, first, rows):
    row = first + lax.broadcasted_iota(jnp.int32, (rows, targets.shape[1]), 0)
    return jnp.where(row == targets, 1.0, 0.0).astype(jnp.bfloat16)


def sublayer_kernel(
    devices, pages, reach, back,
    table_ref, frequency_ref, base_cos_ref, base_sin_ref, local_cos_ref, local_sin_ref, gain_ref,
    tokens_ref, w_kv_ref, w_query_ref, w_out_ref,
    out_ref, cache_out,
    tokens_buf, w_kv_buf, w_query_buf, w_out_buf, normed, key_own, value_own, key_in, value_in,
    tables, kv_rows, send_pages, got_pages, cosine, sine, projected, query, context,
    key_all, value_sum, low_all, right, load_sem,
    table_send, table_recv, page_send, page_recv, kv_send, kv_recv,
):
    me = lax.axis_index("seq")
    heads, rows, head_dim = query.shape
    half = head_dim // 2
    seg_rows = rows // LANES
    loads = [
        pltpu.make_async_copy(source, target, load_sem.at[i])
        for i, (source, target) in enumerate(
            [(tokens_ref, tokens_buf), (w_kv_ref, w_kv_buf), (w_query_ref, w_query_buf), (w_out_ref, w_out_buf)]
        )
    ]
    for load in loads:
        load.start()

    barrier = pltpu.get_barrier_semaphore()

    def greet(k, carry):
        pl.semaphore_signal(
            barrier, inc=1, device_id=(lax.rem(me + k, devices),), device_id_type=MESH
        )
        return carry

    lax.fori_loop(1, devices, greet, 0)

    lane = lax.broadcasted_iota(jnp.int32, (rows, head_dim), 1)
    base_cos, base_sin = base_cos_ref[pl.ds(me, 1), :], base_sin_ref[pl.ds(me, 1), :]
    local_cos, local_sin = local_cos_ref[...], local_sin_ref[...]
    cosine[...] = base_cos * local_cos - base_sin * local_sin
    stream_sin = base_sin * local_cos + base_cos * local_sin
    sine[...] = jnp.where(lane < half, -stream_sin, stream_sin)

    loads[0].wait()
    step = 128

    def norm_tile(i, carry):
        at = pl.ds(pl.multiple_of(i * step, step), step)
        wide = tokens_buf[at, :].astype(jnp.float32)
        mean_square = jnp.mean(wide * wide, -1, keepdims=True)
        normed[at, :] = (wide * lax.rsqrt(mean_square + EPS) * gain_ref[...]).astype(jnp.bfloat16)
        return carry

    lax.fori_loop(0, rows // step, norm_tile, 0)
    loads[1].wait()
    projected[...] = jnp.dot(normed[...], w_kv_buf[...], preferred_element_type=jnp.float32)

    def rotate(v):
        return v * cosine[...] + pltpu.roll(v, half, 1) * sine[...]

    key_own[...] = rotate(projected[:, :head_dim]).T.astype(jnp.bfloat16)
    value_own[...] = projected[:, head_dim:].astype(jnp.bfloat16)

    pl.semaphore_wait(barrier, devices - 1)
    kv_copies = []
    for hop in range(1, reach + 1):
        for part, (source, target) in enumerate([(key_own, key_in), (value_own, value_in)]):
            copy = pltpu.make_async_remote_copy(
                src_ref=source, dst_ref=target.at[reach - hop],
                send_sem=kv_send.at[2 * hop - 2 + part], recv_sem=kv_recv.at[2 * hop - 2 + part],
                device_id=(lax.rem(me + hop, devices),), device_id_type=MESH,
            )
            copy.start()
            kv_copies.append(copy)

    def send_table(k, carry):
        pltpu.make_async_remote_copy(
            src_ref=table_ref, dst_ref=tables.at[k - 1], send_sem=table_send, recv_sem=table_recv,
            device_id=(lax.rem(me + k, devices),), device_id_type=MESH,
        ).start()
        return carry

    lax.fori_loop(1, devices, send_table, 0)
    tables[devices - 1] = table_ref[...]

    loads[2].wait()
    pair = 2 * head_dim
    scale = head_dim ** (-0.5) * math.log2(math.e)

    def query_pair(j, carry):
        columns = pl.ds(pl.multiple_of(j * pair, pair), pair)
        part = jnp.dot(normed[...], w_query_buf[:, columns], preferred_element_type=jnp.float32)
        query[2 * j] = (rotate(part[:, :head_dim]) * scale).astype(jnp.bfloat16)
        query[2 * j + 1] = (rotate(part[:, head_dim:]) * scale).astype(jnp.bfloat16)
        return carry

    lax.fori_loop(0, heads // 2, query_pair, 0)

    table = table_ref[...]
    ids = jnp.concatenate([column_of(table[r : r + 1, :]) for r in range(seg_rows)], 0)
    below = jnp.zeros((rows, LANES), jnp.int32)
    for r in range(seg_rows):
        below = below + jnp.where(table[r : r + 1, :] < ids, 1, 0)
    local_start = jnp.sum(below, 1, keepdims=True)
    owner_column = column_of(table[seg_rows : seg_rows + 1, :])[:pages]
    order = one_hot_rows(spread(owner_column, pages), 0, devices * PAGE)

    blocks = tables.at[pl.ds(0, devices - 1)]
    pltpu.make_async_copy(blocks, blocks, table_recv).wait()
    first_id = table[0:1, 0:1]
    earlier = jnp.zeros((seg_rows, LANES), jnp.int32)
    for k in range(1, min(back, devices - 1) + 1):
        present = jnp.where(me >= k, 1, 0)
        earlier = earlier + jnp.where(tables[k - 1, 0:seg_rows, :] == first_id, present, 0)
    before = jnp.sum(jnp.sum(earlier, 1, keepdims=True), 0, keepdims=True)
    local_index = lax.broadcasted_iota(jnp.int32, (rows, 1), 0)
    start = local_start - jnp.where(ids == first_id, before, 0)
    low = jnp.maximum(start, local_index - (WINDOW - 1)) + reach * rows
    low_all[...] = jnp.broadcast_to(low, low_all.shape)

    cos_part, sin_part = cos_sin((local_index - start).astype(jnp.float32) * frequency_ref[...])
    sin_part = jnp.where(lane < half, -sin_part, sin_part)
    keys = projected[:, :head_dim]
    kv_rows[:, :head_dim] = (keys * cos_part + pltpu.roll(keys, half, 1) * sin_part).astype(jnp.bfloat16)
    kv_rows[:, head_dim:] = value_own[...]
    send_pages[...] = (
        jnp.dot(order, kv_rows[...], preferred_element_type=jnp.float32)
        .astype(jnp.bfloat16)
        .reshape(send_pages.shape)
    )

    def send_page(k, carry):
        to = lax.rem(me + k, devices)
        pltpu.make_async_remote_copy(
            src_ref=send_pages.at[to], dst_ref=got_pages.at[k - 1],
            send_sem=page_send, recv_sem=page_recv,
            device_id=(to,), device_id_type=MESH,
        ).start()
        return carry

    lax.fori_loop(1, devices, send_page, 0)
    got_pages[devices - 1] = send_pages[me]

    value_sum[reach * rows :, :head_dim] = value_own[...]
    value_sum[:, head_dim:] = jnp.ones((value_sum.shape[0], head_dim), jnp.bfloat16)
    key_all[:, reach * rows :] = key_own[...]
    for copy in kv_copies:
        copy.wait()
    for slot in range(reach):
        value_sum[slot * rows : (slot + 1) * rows, :head_dim] = value_in[slot]
        key_all[:, slot * rows : (slot + 1) * rows] = key_in[slot]
    span = WINDOW + QUERY_TILE
    extra = reach * rows
    mark = (QUERY_TILE, QUERY_TILE)
    same = lax.broadcasted_iota(jnp.int32, mark, 0) == lax.broadcasted_iota(jnp.int32, mark, 1)
    unit = jnp.where(same, 1.0, 0.0).astype(jnp.bfloat16)
    units = jnp.concatenate([unit] * HEAD_GROUP, 0)

    def tile(i, carry):
        first = pl.multiple_of(i * QUERY_TILE, QUERY_TILE)
        at = pl.ds(first, QUERY_TILE)
        shape = (QUERY_TILE, span)
        key_row = first + (extra - WINDOW) + lax.broadcasted_iota(jnp.int32, shape, 1)
        query_row = first + extra + lax.broadcasted_iota(jnp.int32, shape, 0)
        bias = jnp.where((key_row >= low_all[at, 0:1]) & (key_row <= query_row), 0.0, -1e30)
        key_at = pl.ds(pl.multiple_of(first + (extra - WINDOW), QUERY_TILE), span)
        right[:head_dim, :] = key_all[:, key_at]
        right[head_dim:, :] = bias.astype(jnp.bfloat16)

        def scores_of(g):
            left = jnp.concatenate([query[g * HEAD_GROUP + j, at, :] for j in range(HEAD_GROUP)], 0)
            return jnp.dot(
                jnp.concatenate([left, units], 1), right[...], preferred_element_type=jnp.float32
            )

        scores = scores_of(0)
        for g in range(heads // HEAD_GROUP):
            following = scores_of(g + 1) if g + 1 < heads // HEAD_GROUP else None
            peak = jnp.max(scores, 1, keepdims=True)
            weights = jnp.exp2(scores - peak).astype(jnp.bfloat16)
            both = jnp.dot(weights, value_sum[key_at, :], preferred_element_type=jnp.float32)
            mixed = (both[:, :head_dim] / both[:, head_dim:]).astype(jnp.bfloat16)
            for j in range(HEAD_GROUP):
                h = g * HEAD_GROUP + j
                context[at, h * head_dim : (h + 1) * head_dim] = mixed[
                    j * QUERY_TILE : (j + 1) * QUERY_TILE
                ]
            scores = following
        return carry

    lax.fori_loop(0, rows // QUERY_TILE, tile, 0)
    loads[3].wait()
    width = 256

    def column(j, carry):
        columns = pl.ds(pl.multiple_of(j * width, width), width)
        out_ref[:, columns] = jnp.dot(
            context[...], w_out_buf[:, columns], preferred_element_type=jnp.float32
        ).astype(jnp.bfloat16)
        return carry

    lax.fori_loop(0, out_ref.shape[1] // width, column, 0)

    owners = tables[:, seg_rows, :]
    slots = tables[:, seg_rows + 1, :]
    slot_column = jnp.sum(jnp.where(owners == me, slots + 1, 0), 1, keepdims=True) - 1
    targets = spread(slot_column, devices)
    pages_in = got_pages.at[pl.ds(0, devices - 1)]
    pltpu.make_async_copy(pages_in, pages_in, page_recv).wait()
    got = got_pages[...].reshape(devices * PAGE, 2 * head_dim)
    chunk = min(512, cache_out.shape[0])
    for c in range(cache_out.shape[0] // chunk):
        place = one_hot_rows(targets, c * chunk, chunk)
        cache_out[c * chunk : (c + 1) * chunk, :] = jnp.dot(
            place, got, preferred_element_type=jnp.float32
        ).astype(jnp.bfloat16)
    pltpu.make_async_copy(blocks, blocks, table_send).wait()
    pltpu.make_async_copy(pages_in, pages_in, page_send).wait()


def body(devices, tokens, norm_gain, w_query, w_key_value, w_out, segment_ids, page_owner, page_slot):
    rows, width = tokens.shape
    head_dim = w_key_value.shape[1] // 2
    heads = w_query.shape[1] // head_dim
    pages = rows // PAGE
    reach = WINDOW // rows
    back = MAXLEN // rows
    bf16, f32 = jnp.bfloat16, jnp.float32
    pad = jnp.full((LANES - pages,), -1, jnp.int32)
    seg_rows = rows // LANES
    table = jnp.concatenate(
        [segment_ids, page_owner, pad, page_slot, pad, jnp.zeros(((6 - seg_rows) * LANES,), jnp.int32)]
    ).reshape(8, LANES)
    half = ROPE_BASE ** (-2.0 * np.arange(head_dim // 2, dtype=np.float64) / head_dim)
    frequency = np.concatenate([half, half])[None, :]
    base = np.arange(devices, dtype=np.float64)[:, None] * rows * frequency
    local = np.arange(rows, dtype=np.float64)[:, None] * frequency
    constants = [
        jnp.asarray(c.astype(np.float32))
        for c in (frequency, np.cos(base), np.sin(base), np.cos(local), np.sin(local))
    ]
    vmem = pl.BlockSpec(memory_space=pltpu.VMEM)
    anywhere = pl.BlockSpec(memory_space=pltpu.HBM)
    dma = pltpu.SemaphoreType.DMA
    total = (reach + 1) * rows
    return pl.pallas_call(
        functools.partial(sublayer_kernel, devices, pages, reach, back),
        out_shape=(
            jax.ShapeDtypeStruct((rows, w_out.shape[1]), bf16),
            jax.ShapeDtypeStruct((devices * PAGE, 2 * head_dim), bf16),
        ),
        in_specs=[vmem] * 7 + [anywhere] * 4,
        out_specs=(vmem, vmem),
        scratch_shapes=[
            pltpu.VMEM((rows, width), bf16),
            pltpu.VMEM(w_key_value.shape, bf16),
            pltpu.VMEM(w_query.shape, bf16),
            pltpu.VMEM(w_out.shape, bf16),
            pltpu.VMEM((rows, width), bf16),
            pltpu.VMEM((head_dim, rows), bf16),
            pltpu.VMEM((rows, head_dim), bf16),
            pltpu.VMEM((reach, head_dim, rows), bf16),
            pltpu.VMEM((reach, rows, head_dim), bf16),
            pltpu.VMEM((devices, 8, LANES), jnp.int32),
            pltpu.VMEM((rows, 2 * head_dim), bf16),
            pltpu.VMEM((devices, PAGE, 2 * head_dim), bf16),
            pltpu.VMEM((devices, PAGE, 2 * head_dim), bf16),
            pltpu.VMEM((rows, head_dim), f32),
            pltpu.VMEM((rows, head_dim), f32),
            pltpu.VMEM((rows, 2 * head_dim), f32),
            pltpu.VMEM((heads, rows, head_dim), bf16),
            pltpu.VMEM((rows, heads * head_dim), bf16),
            pltpu.VMEM((head_dim, total), bf16),
            pltpu.VMEM((total, 2 * head_dim), bf16),
            pltpu.VMEM((rows, LANES), jnp.int32),
            pltpu.VMEM((head_dim + QUERY_TILE, WINDOW + QUERY_TILE), bf16),
            dma((4,)),
            dma, dma, dma, dma,
            dma((2 * reach,)), dma((2 * reach,)),
        ],
        compiler_params=pltpu.CompilerParams(
            collective_id=0, has_side_effects=True, vmem_limit_bytes=56 * 1024 * 1024
        ),
        name="attention_sublayer",
    )(table, *constants, norm_gain.reshape(1, width), tokens, w_key_value, w_query, w_out)


def solution(mesh):
    placed = (P("seq", None), P(), P(), P(), P(), P("seq"), P("seq"), P("seq"))
    return jax.shard_map(
        functools.partial(body, mesh.shape["seq"]),
        mesh=mesh,
        in_specs=placed,
        out_specs=(P("seq", None), P("seq", None)),
        check_vma=False,
    )
```

time: 56.6 us -> 45.7 us (0.81)
  Pallas kernels: 50.3 us -> 38.7 us
  local copies, waits for them, and re-layouts: 5.37 us -> 6.05 us
    pallas_call x2 -> x1, Pallas kernels: 50.3 us -> 38.7 us  [body(): pl.pallas_call(functools.partial(sublayer_kernel, devices, pages, reach,...]
    reshape x1, local copies, waits for them, and re-layouts: 0.7 us -> 1.29 us  [body(): norm_gain.reshape(1, width)]
    concatenate x1, local copies, waits for them, and re-layouts: 0.77 us -> 1.35 us  [body(): jnp.concatenate([segment_ids, page_owner, pad, page_slot, pad, jnp.zeros(...]
    unnamed x7 -> x4, local copies, waits for them, and re-layouts: 3.9 us -> 3.4 us
where the time goes in v2:
time: 45.7 us; the launch traced here: 45.4 us
  Pallas kernels  38.7 us (85%)
  local copies, waits for them, and re-layouts  6.05 us (13%)
  between operations  0.66 us (1%)
    pallas_call x1, Pallas kernels, body(): pl.pallas_call(functools.partial(sublayer_kernel, devices, pages, reach,...  38.7 us
    unnamed x4, local copies, waits for them, and re-layouts  3.4 us
    concatenate x1, local copies, waits for them, and re-layouts, body(): jnp.concatenate([segment_ids, page_owner, pad, page_slot, pad, jnp.zeros(...  1.35 us
    reshape x1, local copies, waits for them, and re-layouts, body(): norm_gain.reshape(1, width)  1.29 us

profile of v2, /device:TPU:0, one launch (start us, length us, event | category | flops | bytes accessed | tf_op | source)
XLA Modules:
  0.0 45.4 jit_solution(15583053065662100034)
XLA Ops:
  0.6 1.4 %concatenate.3 = s32[1024]{0:T(1024)} concatenate(s32[512]{0:T(512)} %param.18, s32[32]{0:T(128)} %param.19, s32[96]{0:T(128)S(1)} %broadcast_in_dim.6, s32[32]{0:T(128)} %param.20, s32[96]{0:T(128)S(1)} %broadcast_in_dim.6, s32[256]{0:T(256)S(1)} %broadcast_in_dim.7), dimensions={0} | concatenate | bytes 8192 | tf_op jit(solution)/shard_map/concatenate | solution.py:287
  2.0 1.3 %reshape.11.gain_ref = f32[1,1536]{1,0:T(1,128)} reshape(f32[1536]{0:T(1024)} %param.14) | data formatting | bytes 12288 | tf_op jit(solution)/shard_map/reshape | solution.py:341
  3.3 38.7 %attention_sublayer.1 = (bf16[512,1536]{1,0:T(8,128)(2,1)}, bf16[512,256]{1,0:T(8,128)(2,1)}) custom-call(s32[8,128]{1,0:T(8,128)} %bitcast.1, f32[1,128]{1,0:T(1,128)} %constant.14.clone.frequency_ref, f32[32,128]{1,0:T(8,128)} %constant.15.clone.base_cos_ref, f32[32,128]{1,0:T(8,128)} %constant.16.clone.base_sin_ref, ...), custom_call_target="tpu_custom_call" | custom-call | tf_op jit(solution)/shard_map/attention_sublayer/pallas_call | solution.py:302
  42.0 0.0 copy-start
  42.0 2.7 %copy.17 = bf16[512,1536]{1,0:T(8,128)(2,1)} copy(bf16[512,1536]{1,0:T(8,128)(2,1)} %get-tuple-element.4) | data formatting | bytes 3145728
  44.7 0.0 copy-done
  44.7 0.7 %copy.18 = bf16[512,256]{1,0:T(8,128)(2,1)} copy(bf16[512,256]{1,0:T(8,128)(2,1)S(1)} %copy-done) | data formatting | bytes 524288
  (2 shorter events, 0.0 us)
Async XLA Ops:
  42.0 2.7 %copy-start = (bf16[512,256]{1,0:T(8,128)(2,1)S(1)}, bf16[512,256]{1,0:T(8,128)(2,1)}, u32[]{:S(2)}) copy-start(bf16[512,256]{1,0:T(8,128)(2,1)} %get-tuple-element.5) | copy-start | bytes 786436

commit v3 on v2

--- a/solution.py
+++ b/solution.py
@@ -59,11 +59,11 @@
 
 def sublayer_kernel(
     devices, pages, reach, back,
-    table_ref, frequency_ref, base_cos_ref, base_sin_ref, local_cos_ref, local_sin_ref, gain_ref,
-    tokens_ref, w_kv_ref, w_query_ref, w_out_ref,
-    out_ref, cache_out,
-    tokens_buf, w_kv_buf, w_query_buf, w_out_buf, normed, key_own, value_own, key_in, value_in,
-    tables, kv_rows, send_pages, got_pages, cosine, sine, projected, query, context,
+    ids_ref, owner_ref, slot_ref, frequency_ref, gain_ref, trig_ref,
+    tokens_ref, w_kv_ref, w_query_ref,
+    context, pages_out, target_out,
+    trig, tokens_buf, w_kv_buf, w_query_buf, normed, key_own, value_own, key_in, value_in,
+    table_ref, tables, kv_rows, send_pages, got_pages, cosine, sine, projected, query,
     key_all, value_sum, low_all, right, load_sem,
     table_send, table_recv, page_send, page_recv, kv_send, kv_recv,
 ):
@@ -74,7 +74,7 @@
     loads = [
         pltpu.make_async_copy(source, target, load_sem.at[i])
         for i, (source, target) in enumerate(
-            [(tokens_ref, tokens_buf), (w_kv_ref, w_kv_buf), (w_query_ref, w_query_buf), (w_out_ref, w_out_buf)]
+            [(tokens_ref, tokens_buf), (w_kv_ref, w_kv_buf), (w_query_ref, w_query_buf), (trig_ref, trig)]
         )
     ]
     for load in loads:
@@ -90,13 +90,11 @@
 
     lax.fori_loop(1, devices, greet, 0)
 
-    lane = lax.broadcasted_iota(jnp.int32, (rows, head_dim), 1)
-    base_cos, base_sin = base_cos_ref[pl.ds(me, 1), :], base_sin_ref[pl.ds(me, 1), :]
-    local_cos, local_sin = local_cos_ref[...], local_sin_ref[...]
-    cosine[...] = base_cos * local_cos - base_sin * local_sin
-    stream_sin = base_sin * local_cos + base_cos * local_sin
-    sine[...] = jnp.where(lane < half, -stream_sin, stream_sin)
-
+    table_ref[...] = jnp.full(table_ref.shape, -1, jnp.int32)
+    table_ref[0:seg_rows, :] = ids_ref[...]
+    table_ref[seg_rows : seg_rows + 1, 0:pages] = owner_ref[...]
+    table_ref[seg_rows + 1 : seg_rows + 2, 0:pages] = slot_ref[...]
+    gain = jnp.concatenate([gain_ref[r : r + 1, :] for r in range(gain_ref.shape[0])], 1)
     loads[0].wait()
     step = 128
 
@@ -104,13 +102,21 @@
         at = pl.ds(pl.multiple_of(i * step, step), step)
         wide = tokens_buf[at, :].astype(jnp.float32)
         mean_square = jnp.mean(wide * wide, -1, keepdims=True)
-        normed[at, :] = (wide * lax.rsqrt(mean_square + EPS) * gain_ref[...]).astype(jnp.bfloat16)
+        normed[at, :] = (wide * lax.rsqrt(mean_square + EPS) * gain).astype(jnp.bfloat16)
         return carry
 
     lax.fori_loop(0, rows // step, norm_tile, 0)
     loads[1].wait()
     projected[...] = jnp.dot(normed[...], w_kv_buf[...], preferred_element_type=jnp.float32)
 
+    loads[3].wait()
+    lane = lax.broadcasted_iota(jnp.int32, (rows, head_dim), 1)
+    base_cos, base_sin = trig[pl.ds(2 * rows + me, 1), :], trig[pl.ds(2 * rows + devices + me, 1), :]
+    local_cos, local_sin = trig[0:rows, :], trig[rows : 2 * rows, :]
+    cosine[...] = base_cos * local_cos - base_sin * local_sin
+    stream_sin = base_sin * local_cos + base_cos * local_sin
+    sine[...] = jnp.where(lane < half, -stream_sin, stream_sin)
+
     def rotate(v):
         return v * cosine[...] + pltpu.roll(v, half, 1) * sine[...]
 
@@ -118,16 +124,27 @@
     value_own[...] = projected[:, head_dim:].astype(jnp.bfloat16)
 
     pl.semaphore_wait(barrier, devices - 1)
-    kv_copies = []
-    for hop in range(1, reach + 1):
-        for part, (source, target) in enumerate([(key_own, key_in), (value_own, value_in)]):
-            copy = pltpu.make_async_remote_copy(
+    def kv_hop(hop):
+        return [
+            pltpu.make_async_remote_copy(
                 src_ref=source, dst_ref=target.at[reach - hop],
                 send_sem=kv_send.at[2 * hop - 2 + part], recv_sem=kv_recv.at[2 * hop - 2 + part],
                 device_id=(lax.rem(me + hop, devices),), device_id_type=MESH,
             )
-            copy.start()
-            kv_copies.append(copy)
+            for part, (source, target) in enumerate([(key_own, key_in), (value_own, value_in)])
+        ]
+
+    for hop in range(1, reach + 1):
+
+        @pl.when(me + hop < devices)
+        def _():
+            for copy in kv_hop(hop):
+                copy.start()
+
+        @pl.when(me < hop)
+        def _():
+            key_in[reach - hop] = jnp.zeros_like(key_own)
+            value_in[reach - hop] = jnp.zeros_like(value_own)
 
     def send_table(k, carry):
         pltpu.make_async_remote_copy(
@@ -200,8 +217,13 @@
     value_sum[reach * rows :, :head_dim] = value_own[...]
     value_sum[:, head_dim:] = jnp.ones((value_sum.shape[0], head_dim), jnp.bfloat16)
     key_all[:, reach * rows :] = key_own[...]
-    for copy in kv_copies:
-        copy.wait()
+    for hop in range(1, reach + 1):
+
+        @pl.when(me >= hop)
+        def _():
+            for copy in kv_hop(hop):
+                copy.wait_recv()
+
     for slot in range(reach):
         value_sum[slot * rows : (slot + 1) * rows, :head_dim] = value_in[slot]
         key_all[:, slot * rows : (slot + 1) * rows] = key_in[slot]
@@ -245,33 +267,38 @@
         return carry
 
     lax.fori_loop(0, rows // QUERY_TILE, tile, 0)
-    loads[3].wait()
-    width = 256
-
-    def column(j, carry):
-        columns = pl.ds(pl.multiple_of(j * width, width), width)
-        out_ref[:, columns] = jnp.dot(
-            context[...], w_out_buf[:, columns], preferred_element_type=jnp.float32
-        ).astype(jnp.bfloat16)
-        return carry
-
-    lax.fori_loop(0, out_ref.shape[1] // width, column, 0)
 
     owners = tables[:, seg_rows, :]
     slots = tables[:, seg_rows + 1, :]
     slot_column = jnp.sum(jnp.where(owners == me, slots + 1, 0), 1, keepdims=True) - 1
-    targets = spread(slot_column, devices)
+    target_out[...] = spread(slot_column, devices)
     pages_in = got_pages.at[pl.ds(0, devices - 1)]
     pltpu.make_async_copy(pages_in, pages_in, page_recv).wait()
-    got = got_pages[...].reshape(devices * PAGE, 2 * head_dim)
-    chunk = min(512, cache_out.shape[0])
-    for c in range(cache_out.shape[0] // chunk):
-        place = one_hot_rows(targets, c * chunk, chunk)
-        cache_out[c * chunk : (c + 1) * chunk, :] = jnp.dot(
-            place, got, preferred_element_type=jnp.float32
-        ).astype(jnp.bfloat16)
+    pages_out[...] = got_pages[...].reshape(devices * PAGE, 2 * head_dim)
+    for hop in range(1, reach + 1):
+
+        @pl.when(me + hop < devices)
+        def _():
+            for copy in kv_hop(hop):
+                copy.wait_send()
+
     pltpu.make_async_copy(blocks, blocks, table_send).wait()
     pltpu.make_async_copy(pages_in, pages_in, page_send).wait()
+
+
+def output_kernel(context_ref, w_out_ref, pages_ref, target_ref, out_ref, cache_out):
+    out_ref[...] = jnp.dot(
+        context_ref[...], w_out_ref[...], preferred_element_type=jnp.float32
+    ).astype(jnp.bfloat16)
+
+    @pl.when(pl.program_id(0) == 0)
+    def _():
+        chunk = min(512, cache_out.shape[0])
+        for c in range(cache_out.shape[0] // chunk):
+            place = one_hot_rows(target_ref[...], c * chunk, chunk)
+            cache_out[c * chunk : (c + 1) * chunk, :] = jnp.dot(
+                place, pages_ref[...], preferred_element_type=jnp.float32
+            ).astype(jnp.bfloat16)
 
 
 def body(devices, tokens, norm_gain, w_query, w_key_value, w_out, segment_ids, page_owner, page_slot):
@@ -282,41 +309,37 @@
     reach = WINDOW // rows
     back = MAXLEN // rows
     bf16, f32 = jnp.bfloat16, jnp.float32
-    pad = jnp.full((LANES - pages,), -1, jnp.int32)
-    seg_rows = rows // LANES
-    table = jnp.concatenate(
-        [segment_ids, page_owner, pad, page_slot, pad, jnp.zeros(((6 - seg_rows) * LANES,), jnp.int32)]
-    ).reshape(8, LANES)
     half = ROPE_BASE ** (-2.0 * np.arange(head_dim // 2, dtype=np.float64) / head_dim)
     frequency = np.concatenate([half, half])[None, :]
     base = np.arange(devices, dtype=np.float64)[:, None] * rows * frequency
     local = np.arange(rows, dtype=np.float64)[:, None] * frequency
-    constants = [
-        jnp.asarray(c.astype(np.float32))
-        for c in (frequency, np.cos(base), np.sin(base), np.cos(local), np.sin(local))
-    ]
+    trig = jnp.asarray(
+        np.concatenate([np.cos(local), np.sin(local), np.cos(base), np.sin(base)]).astype(np.float32)
+    )
     vmem = pl.BlockSpec(memory_space=pltpu.VMEM)
     anywhere = pl.BlockSpec(memory_space=pltpu.HBM)
     dma = pltpu.SemaphoreType.DMA
     total = (reach + 1) * rows
-    return pl.pallas_call(
+    context, got_pages, targets = pl.pallas_call(
         functools.partial(sublayer_kernel, devices, pages, reach, back),
         out_shape=(
-            jax.ShapeDtypeStruct((rows, w_out.shape[1]), bf16),
+            jax.ShapeDtypeStruct((rows, heads * head_dim), bf16),
             jax.ShapeDtypeStruct((devices * PAGE, 2 * head_dim), bf16),
+            jax.ShapeDtypeStruct((1, devices * PAGE), jnp.int32),
         ),
-        in_specs=[vmem] * 7 + [anywhere] * 4,
-        out_specs=(vmem, vmem),
+        in_specs=[vmem] * 5 + [anywhere] * 4,
+        out_specs=(vmem, vmem, vmem),
         scratch_shapes=[
+            pltpu.VMEM(trig.shape, f32),
             pltpu.VMEM((rows, width), bf16),
             pltpu.VMEM(w_key_value.shape, bf16),
             pltpu.VMEM(w_query.shape, bf16),
-            pltpu.VMEM(w_out.shape, bf16),
             pltpu.VMEM((rows, width), bf16),
             pltpu.VMEM((head_dim, rows), bf16),
             pltpu.VMEM((rows, head_dim), bf16),
             pltpu.VMEM((reach, head_dim, rows), bf16),
             pltpu.VMEM((reach, rows, head_dim), bf16),
+            pltpu.VMEM((8, LANES), jnp.int32),
             pltpu.VMEM((devices, 8, LANES), jnp.int32),
             pltpu.VMEM((rows, 2 * head_dim), bf16),
             pltpu.VMEM((devices, PAGE, 2 * head_dim), bf16),
@@ -325,7 +348,6 @@
             pltpu.VMEM((rows, head_dim), f32),
             pltpu.VMEM((rows, 2 * head_dim), f32),
             pltpu.VMEM((heads, rows, head_dim), bf16),
-            pltpu.VMEM((rows, heads * head_dim), bf16),
             pltpu.VMEM((head_dim, total), bf16),
             pltpu.VMEM((total, 2 * head_dim), bf16),
             pltpu.VMEM((rows, LANES), jnp.int32),
@@ -338,7 +360,31 @@
             collective_id=0, has_side_effects=True, vmem_limit_bytes=56 * 1024 * 1024
         ),
         name="attention_sublayer",
-    )(table, *constants, norm_gain.reshape(1, width), tokens, w_key_value, w_query, w_out)
+    )(
+        segment_ids.reshape(rows // LANES, LANES), page_owner.reshape(1, pages), page_slot.reshape(1, pages),
+        jnp.asarray(frequency.astype(np.float32)), norm_gain.reshape(width // LANES, LANES),
+        trig, tokens, w_key_value, w_query,
+    )
+    tile = 256
+    inner, wide = w_out.shape
+    whole = lambda shape: pl.BlockSpec(shape, lambda j: (0, 0))
+    return pl.pallas_call(
+        output_kernel,
+        grid=(wide // tile,),
+        out_shape=(
+            jax.ShapeDtypeStruct((rows, wide), bf16),
+            jax.ShapeDtypeStruct(got_pages.shape, bf16),
+        ),
+        in_specs=[
+            whole((rows, inner)),
+            pl.BlockSpec((inner, tile), lambda j: (0, j)),
+            whole(got_pages.shape),
+            whole(targets.shape),
+        ],
+        out_specs=(pl.BlockSpec((rows, tile), lambda j: (0, j)), whole(got_pages.shape)),
+        compiler_params=pltpu.CompilerParams(vmem_limit_bytes=24 * 1024 * 1024),
+        name="output_projection",
+    )(context, w_out, got_pages, targets)
 
 
 def solution(mesh):

time: 45.7 us -> 42.6 us (0.932)
  local copies, waits for them, and re-layouts: 6.05 us -> 3.03 us
    pallas_call x1, Pallas kernels: 38.7 us -> 33.7 us  [body(): pl.pallas_call(functools.partial(sublayer_kernel, devices, pages, reach,...]
    pallas_call x0 -> x1, Pallas kernels: none -> 5.02 us  [body(): pl.pallas_call(output_kernel, grid=(wide // tile,), out_shape=(jax.ShapeD...]
    concatenate x1 -> x0, local copies, waits for them, and re-layouts: 1.35 us -> none  [body(): jnp.concatenate([segment_ids, page_owner, pad, page_slot, pad, jnp.zeros(...]
    reshape x1 -> x0, local copies, waits for them, and re-layouts: 1.29 us -> none  [body(): norm_gain.reshape(1, width)]
    unnamed x4 -> x8, local copies, waits for them, and re-layouts: 3.4 us -> 3.03 us
where the time goes in v3:
time: 42.6 us; the launch traced here: 42.4 us
  Pallas kernels  38.7 us (91%)
  local copies, waits for them, and re-layouts  3.03 us (7%)
  between operations  0.67 us (2%)
    pallas_call x1, Pallas kernels, body(): pl.pallas_call(functools.partial(sublayer_kernel, devices, pages, reach,...  33.7 us
    pallas_call x1, Pallas kernels, body(): pl.pallas_call(output_kernel, grid=(wide // tile,), out_shape=(jax.ShapeD...  5.02 us
    unnamed x8, local copies, waits for them, and re-layouts  3.03 us

profile of v3, /device:TPU:0, one launch (start us, length us, event | category | flops | bytes accessed | tf_op | source)
XLA Modules:
  0.0 42.4 jit_solution(7095002963601101235)
XLA Ops:
  0.6 0.0 copy-start
  0.6 33.7 %attention_sublayer.1 = (bf16[512,1536]{1,0:T(8,128)(2,1)}, bf16[512,256]{1,0:T(8,128)(2,1)}, s32[1,512]{1,0:T(1,128)}) custom-call(s32[4,128]{1,0:T(4,128)} %bitcast.5, s32[1,32]{1,0:T(1,128)} %bitcast.6, s32[1,32]{1,0:T(1,128)} %bitcast.7, f32[1,128]{1,0:T(1,128)} %constant.5.clone.frequency_ref, f32[12,128]{1,0:T(8,128)} %bitcast.4, ...), custom_call_target="tpu_custom_call" | custom-call | tf_op jit(solution)/shard_map/attention_sublayer/pallas_call | solution.py:323
  34.3 0.0 copy-done
  34.3 0.0 copy-start.1
  34.3 1.4 %copy-done.1 = bf16[512,1536]{1,0:T(8,128)(2,1)S(1)} copy-done((bf16[512,1536]{1,0:T(8,128)(2,1)S(1)}, bf16[512,1536]{1,0:T(8,128)(2,1)}, u32[]{:S(2)}) %copy-start.1) | copy-done | bytes 1572888
  35.7 0.0 copy-start.2
  35.7 0.9 %copy-done.2 = bf16[512,256]{1,0:T(8,128)(2,1)S(1)} copy-done((bf16[512,256]{1,0:T(8,128)(2,1)S(1)}, bf16[512,256]{1,0:T(8,128)(2,1)}, u32[]{:S(2)}) %copy-start.2) | copy-done | bytes 262168
  36.7 0.0 copy-start.3
  36.7 0.7 %copy-done.3 = s32[1,512]{1,0:T(1,128)S(1)} copy-done((s32[1,512]{1,0:T(1,128)S(1)}, s32[1,512]{1,0:T(1,128)}, u32[]{:S(2)}) %copy-start.3) | copy-done | bytes 2072
  37.4 5.0 %output_projection.1 = (bf16[512,1536]{1,0:T(8,128)(2,1)}, bf16[512,256]{1,0:T(8,128)(2,1)}) custom-call(bf16[512,1536]{1,0:T(8,128)(2,1)S(1)} %copy-done.1, bf16[1536,1536]{1,0:T(8,128)(2,1)S(1)} %copy-done, bf16[512,256]{1,0:T(8,128)(2,1)S(1)} %copy-done.2, s32[1,512]{1,0:T(1,128)S(1)} %copy-done.3), custom_call_target="tpu_custom_call" | custom-call | tf_op jit(solution)/shard_map/output_projection/pallas_call | solution.py:371
Async XLA Ops:
  0.6 33.7 %copy-start = (bf16[1536,1536]{1,0:T(8,128)(2,1)S(1)}, bf16[1536,1536]{1,0:T(8,128)(2,1)}, u32[]{:S(2)}) copy-start(bf16[1536,1536]{1,0:T(8,128)(2,1)} %w_out_ref.1) | copy-start | bytes 14155780
  34.3 1.4 %copy-start.1 = (bf16[512,1536]{1,0:T(8,128)(2,1)S(1)}, bf16[512,1536]{1,0:T(8,128)(2,1)}, u32[]{:S(2)}) copy-start(bf16[512,1536]{1,0:T(8,128)(2,1)} %get-tuple-element.5.context_ref) | copy-start | bytes 4718596
  35.7 0.9 %copy-start.2 = (bf16[512,256]{1,0:T(8,128)(2,1)S(1)}, bf16[512,256]{1,0:T(8,128)(2,1)}, u32[]{:S(2)}) copy-start(bf16[512,256]{1,0:T(8,128)(2,1)} %get-tuple-element.6.pages_ref) | copy-start | bytes 786436
  36.7 0.7 %copy-start.3 = (s32[1,512]{1,0:T(1,128)S(1)}, s32[1,512]{1,0:T(1,128)}, u32[]{:S(2)}) copy-start(s32[1,512]{1,0:T(1,128)} %get-tuple-element.7.target_ref) | copy-start | bytes 6148

commit v4 on v3

--- a/solution.py
+++ b/solution.py
@@ -16,7 +16,7 @@
 ROPE_BASE = 10000.0
 LANES = 128
 QUERY_TILE = 128
-HEAD_GROUP = 2
+HEAD_GROUP = 4
 MESH = pl.DeviceIdType.MESH
 
 
@@ -64,7 +64,7 @@
     context, pages_out, target_out,
     trig, tokens_buf, w_kv_buf, w_query_buf, normed, key_own, value_own, key_in, value_in,
     table_ref, tables, kv_rows, send_pages, got_pages, cosine, sine, projected, query,
-    key_all, value_sum, low_all, right, load_sem,
+    key_all, value_sum, low_all, right, scores_even, scores_odd, load_sem,
     table_send, table_recv, page_send, page_recv, kv_send, kv_recv,
 ):
     me = lax.axis_index("seq")
@@ -214,9 +214,27 @@
     lax.fori_loop(1, devices, send_page, 0)
     got_pages[devices - 1] = send_pages[me]
 
-    value_sum[reach * rows :, :head_dim] = value_own[...]
+    span = WINDOW + QUERY_TILE
+    extra = reach * rows
+    tiles = rows // QUERY_TILE
+
+    def mask_tile(i, carry):
+        first = pl.multiple_of(i * QUERY_TILE, QUERY_TILE)
+        shape = (QUERY_TILE, span)
+        key_row = first + (extra - WINDOW) + lax.broadcasted_iota(jnp.int32, shape, 1)
+        query_row = first + extra + lax.broadcasted_iota(jnp.int32, shape, 0)
+        seen = (key_row >= low_all[pl.ds(first, QUERY_TILE), 0:1]) & (key_row <= query_row)
+        right[i, head_dim:, :] = jnp.where(seen, 0.0, -1e30).astype(jnp.bfloat16)
+        return carry
+
+    lax.fori_loop(0, tiles, mask_tile, 0)
+    value_sum[extra:, :head_dim] = value_own[...]
     value_sum[:, head_dim:] = jnp.ones((value_sum.shape[0], head_dim), jnp.bfloat16)
-    key_all[:, reach * rows :] = key_own[...]
+    key_all[:, extra:] = key_own[...]
+    mark = (QUERY_TILE, QUERY_TILE)
+    same = lax.broadcasted_iota(jnp.int32, mark, 0) == lax.broadcasted_iota(jnp.int32, mark, 1)
+    unit = jnp.where(same, 1.0, 0.0).astype(jnp.bfloat16)
+    units = jnp.concatenate([unit] * HEAD_GROUP, 0)
     for hop in range(1, reach + 1):
 
         @pl.when(me >= hop)
@@ -227,46 +245,49 @@
     for slot in range(reach):
         value_sum[slot * rows : (slot + 1) * rows, :head_dim] = value_in[slot]
         key_all[:, slot * rows : (slot + 1) * rows] = key_in[slot]
-    span = WINDOW + QUERY_TILE
-    extra = reach * rows
-    mark = (QUERY_TILE, QUERY_TILE)
-    same = lax.broadcasted_iota(jnp.int32, mark, 0) == lax.broadcasted_iota(jnp.int32, mark, 1)
-    unit = jnp.where(same, 1.0, 0.0).astype(jnp.bfloat16)
-    units = jnp.concatenate([unit] * HEAD_GROUP, 0)
-
-    def tile(i, carry):
+    for i in range(tiles):
+        first = i * QUERY_TILE + extra - WINDOW
+        right[i, :head_dim, :] = key_all[:, first : first + span]
+
+    groups = heads // HEAD_GROUP
+    stages = tiles * groups
+
+    def put_scores(n, target):
+        i, g = lax.div(n, groups), lax.rem(n, groups)
+        at = pl.ds(pl.multiple_of(i * QUERY_TILE, QUERY_TILE), QUERY_TILE)
+        left = jnp.concatenate([query[g * HEAD_GROUP + j, at, :] for j in range(HEAD_GROUP)], 0)
+        target[...] = jnp.dot(
+            jnp.concatenate([left, units], 1), right[i], preferred_element_type=jnp.float32
+        )
+
+    def attend(n, source):
+        i, g = lax.div(n, groups), lax.rem(n, groups)
         first = pl.multiple_of(i * QUERY_TILE, QUERY_TILE)
-        at = pl.ds(first, QUERY_TILE)
-        shape = (QUERY_TILE, span)
-        key_row = first + (extra - WINDOW) + lax.broadcasted_iota(jnp.int32, shape, 1)
-        query_row = first + extra + lax.broadcasted_iota(jnp.int32, shape, 0)
-        bias = jnp.where((key_row >= low_all[at, 0:1]) & (key_row <= query_row), 0.0, -1e30)
-        key_at = pl.ds(pl.multiple_of(first + (extra - WINDOW), QUERY_TILE), span)
-        right[:head_dim, :] = key_all[:, key_at]
-        right[head_dim:, :] = bias.astype(jnp.bfloat16)
-
-        def scores_of(g):
-            left = jnp.concatenate([query[g * HEAD_GROUP + j, at, :] for j in range(HEAD_GROUP)], 0)
-            return jnp.dot(
-                jnp.concatenate([left, units], 1), right[...], preferred_element_type=jnp.float32
-            )
-
-        scores = scores_of(0)
-        for g in range(heads // HEAD_GROUP):
-            following = scores_of(g + 1) if g + 1 < heads // HEAD_GROUP else None
-            peak = jnp.max(scores, 1, keepdims=True)
-            weights = jnp.exp2(scores - peak).astype(jnp.bfloat16)
-            both = jnp.dot(weights, value_sum[key_at, :], preferred_element_type=jnp.float32)
-            mixed = (both[:, :head_dim] / both[:, head_dim:]).astype(jnp.bfloat16)
-            for j in range(HEAD_GROUP):
-                h = g * HEAD_GROUP + j
-                context[at, h * head_dim : (h + 1) * head_dim] = mixed[
-                    j * QUERY_TILE : (j + 1) * QUERY_TILE
-                ]
-            scores = following
-        return carry
-
-    lax.fori_loop(0, rows // QUERY_TILE, tile, 0)
+        scores = source[...]
+        peak = jnp.max(scores, 1, keepdims=True)
+        weights = jnp.exp2(scores - peak).astype(jnp.bfloat16)
+        values = value_sum[pl.ds(pl.multiple_of(first + (extra - WINDOW), QUERY_TILE), span), :]
+        both = jnp.dot(weights, values, preferred_element_type=jnp.float32)
+        mixed = (both[:, :head_dim] / both[:, head_dim:]).astype(jnp.bfloat16)
+        for j in range(HEAD_GROUP):
+            column = pl.multiple_of((g * HEAD_GROUP + j) * head_dim, head_dim)
+            context[pl.ds(first, QUERY_TILE), pl.ds(column, head_dim)] = mixed[
+                j * QUERY_TILE : (j + 1) * QUERY_TILE
+            ]
+
+    put_scores(jnp.int32(0), scores_even)
+
+    def two_stages(k, carry):
+        put_scores(2 * k + 1, scores_odd)
+        attend(2 * k, scores_even)
+        put_scores(2 * k + 2, scores_even)
+        attend(2 * k + 1, scores_odd)
+        return carry
+
+    lax.fori_loop(0, stages // 2 - 1, two_stages, 0)
+    put_scores(jnp.int32(stages - 1), scores_odd)
+    attend(jnp.int32(stages - 2), scores_even)
+    attend(jnp.int32(stages - 1), scores_odd)
 
     owners = tables[:, seg_rows, :]
     slots = tables[:, seg_rows + 1, :]
@@ -351,7 +372,9 @@
             pltpu.VMEM((head_dim, total), bf16),
             pltpu.VMEM((total, 2 * head_dim), bf16),
             pltpu.VMEM((rows, LANES), jnp.int32),
-            pltpu.VMEM((head_dim + QUERY_TILE, WINDOW + QUERY_TILE), bf16),
+            pltpu.VMEM((rows // QUERY_TILE, head_dim + QUERY_TILE, WINDOW + QUERY_TILE), bf16),
+            pltpu.VMEM((HEAD_GROUP * QUERY_TILE, WINDOW + QUERY_TILE), f32),
+            pltpu.VMEM((HEAD_GROUP * QUERY_TILE, WINDOW + QUERY_TILE), f32),
             dma((4,)),
             dma, dma, dma, dma,
             dma((2 * reach,)), dma((2 * reach,)),
@@ -365,7 +388,7 @@
         jnp.asarray(frequency.astype(np.float32)), norm_gain.reshape(width // LANES, LANES),
         trig, tokens, w_key_value, w_query,
     )
-    tile = 256
+    tile = 512
     inner, wide = w_out.shape
     whole = lambda shape: pl.BlockSpec(shape, lambda j: (0, 0))
     return pl.pallas_call(
@@ -382,7 +405,7 @@
             whole(targets.shape),
         ],
         out_specs=(pl.BlockSpec((rows, tile), lambda j: (0, j)), whole(got_pages.shape)),
-        compiler_params=pltpu.CompilerParams(vmem_limit_bytes=24 * 1024 * 1024),
+        compiler_params=pltpu.CompilerParams(vmem_limit_bytes=60 * 1024 * 1024),
         name="output_projection",
     )(context, w_out, got_pages, targets)
 

time: 42.6 us -> 40.5 us (0.951)
  local copies, waits for them, and re-layouts: 3.03 us -> 0 us
  Pallas kernels: 38.7 us -> 39.7 us
    unnamed x8 -> x0, local copies, waits for them, and re-layouts: 3.03 us -> none
    pallas_call x1, Pallas kernels: 5.02 us -> 6.66 us  [body(): pl.pallas_call(output_kernel, grid=(wide // tile,), out_shape=(jax.ShapeD...]
    pallas_call x1, Pallas kernels: 33.7 us -> 33 us  [body(): pl.pallas_call(functools.partial(sublayer_kernel, devices, pages, reach,...]
where the time goes in v4:
time: 40.5 us; the launch traced here: 40.3 us
  Pallas kernels  39.7 us (98%)
  between operations  0.64 us (2%)
    pallas_call x1, Pallas kernels, body(): pl.pallas_call(functools.partial(sublayer_kernel, devices, pages, reach,...  33 us
    pallas_call x1, Pallas kernels, body(): pl.pallas_call(output_kernel, grid=(wide // tile,), out_shape=(jax.ShapeD...  6.66 us

profile of v4, /device:TPU:0, one launch (start us, length us, event | category | flops | bytes accessed | tf_op | source)
XLA Modules:
  0.0 40.3 jit_solution(16539986315301702060)
XLA Ops:
  0.6 33.0 %attention_sublayer.1 = (bf16[512,1536]{1,0:T(8,128)(2,1)}, bf16[512,256]{1,0:T(8,128)(2,1)}, s32[1,512]{1,0:T(1,128)}) custom-call(s32[4,128]{1,0:T(4,128)} %bitcast.5, s32[1,32]{1,0:T(1,128)} %bitcast.6, s32[1,32]{1,0:T(1,128)} %bitcast.7, f32[1,128]{1,0:T(1,128)} %constant.5.clone.frequency_ref, f32[12,128]{1,0:T(8,128)} %bitcast.4, ...), custom_call_target="tpu_custom_call" | custom-call | tf_op jit(solution)/shard_map/attention_sublayer/pallas_call | solution.py:344
  33.7 6.7 %output_projection.1 = (bf16[512,1536]{1,0:T(8,128)(2,1)}, bf16[512,256]{1,0:T(8,128)(2,1)}) custom-call(bf16[512,1536]{1,0:T(8,128)(2,1)} %get-tuple-element.5.context_ref, bf16[1536,1536]{1,0:T(8,128)(2,1)} %w_out_ref.1, bf16[512,256]{1,0:T(8,128)(2,1)} %get-tuple-element.6.pages_ref, s32[1,512]{1,0:T(1,128)} %get-tuple-element.7.target_ref), custom_call_target="tpu_custom_call" | custom-call | tf_op jit(solution)/shard_map/output_projection/pallas_call | solution.py:394
